TPU v7x, 32 devices: a whole 2x2x4 slice. The times are simulated.
32 devices in a mesh: slab: 4 (over y, core), dp: 8 (over z, x).
Axes of the slice: x: 2, y: 2, z: 4, core: 2. Of those that a mesh axis runs over, the one named last changes fastest.
Arguments:
- inputs: bfloat16 [8, 32, 24, 64, 128], P('dp', 'slab'), may hold values from -6 to 6
- cotangent: bfloat16 [8, 32, 24, 64, 128], P('dp', 'slab'), may hold values from -4 to 4
- spectral_weight: bfloat16 [16, 256, 4096], P('slab', 'dp'), may hold values from -1.5 to 1.5
- w_in: bfloat16 [64, 256], replicated, may hold values from -0.75 to 0.75
- b_in: float32 [256], replicated, may hold values from -3 to 3
- w_out: bfloat16 [256, 64], replicated, may hold values from -0.375 to 0.375
- b_out: float32 [64], replicated, may hold values from -3 to 3
Outputs:
- grad_inputs: bfloat16 [8, 32, 24, 64, 128], P('dp', 'slab')
- grad_spectral: float32 [16, 256, 4096], P('slab', 'dp')
All inputs are finite; a program needn't handle non-finite values.
Results may differ from a plain program's by a relative error of at most 0.014.
Values may be sent and summed in bfloat16 or wider, within the bound.
A program may use at most 128 MiB of HBM per device.

v0:
```python
import math

import jax
import jax.numpy as jnp
from jax import lax
from jax.sharding import PartitionSpec as P

C = 64
MX = 16
MY = 16
MZ = 16
NX = 32
NY = 24
NZ = 128


root_half = 0.7071067811865476
inv_root_two_pi = 0.3989422804014327


def dft_table(length, kept_count):
    half_kept = kept_count // 2
    positions = jnp.arange(length, dtype=jnp.int32)
    cos_freq = jnp.arange(half_kept, dtype=jnp.int32)
    freqs = jnp.concatenate([cos_freq, cos_freq + 1])[:, None]
    phases = (freqs * positions[None, :] % length).astype(jnp.float32) * (2.0 * math.pi / length)
    values = jnp.concatenate([jnp.cos(phases[:half_kept]), jnp.sin(phases[half_kept:])], axis=0)
    return values.astype(jnp.bfloat16)


def gelu_value(values_in):
    return 0.5 * values_in * (1.0 + jax.scipy.special.erf(values_in * root_half))


def gelu_slope(values_in):
    return (
        0.5 * (1.0 + jax.scipy.special.erf(values_in * root_half))
        + values_in * jnp.exp(-0.5 * values_in * values_in) * inv_root_two_pi
    )


def bdot(form, left, right):
    return jnp.einsum(form, left, right, preferred_element_type=jnp.float32)


def per_device(inputs, cotangent, spectral_weight, w_in, b_in, w_out, b_out):
    slab_count = lax.axis_size("slab")
    group_count = lax.axis_size("dp")
    local_modes = MY // slab_count
    group_modes = MX * MZ // group_count
    crop_count = inputs.shape[0]
    table_x = dft_table(NX, MX)
    table_y = dft_table(NY, MY)
    table_z = dft_table(NZ, MZ)
    factor = 8.0 / (NX * NY * NZ)

    def analyse(samples):
        along_z = bdot("bxycz,kz->bxyck", samples, table_z).astype(jnp.bfloat16)
        along_y = bdot("bxyck,jy->bxjck", along_z, table_y).astype(jnp.bfloat16)
        return bdot(
            "bxjck,ix->bijck",
            lax.all_to_all(along_y, "slab", split_axis=2, concat_axis=1, tiled=True),
            table_x,
        ).astype(jnp.bfloat16)

    def synthesise(coeff_in):
        back_x = bdot("bijck,ix->bxjck", coeff_in, table_x).astype(jnp.bfloat16)
        back_y = bdot(
            "bxjck,jy->bxyck",
            lax.all_to_all(back_x, "slab", split_axis=1, concat_axis=2, tiled=True),
            table_y,
        ).astype(jnp.bfloat16)
        return bdot("bxyck,kz->bxycz", back_y, table_z) * factor

    def send_out(coeff_in):
        ordered = jnp.transpose(coeff_in, (0, 2, 1, 4, 3)).reshape(
            crop_count, local_modes, group_count, group_modes, C
        )
        arrived = lax.all_to_all(ordered, "dp", split_axis=2, concat_axis=0, tiled=True)
        return arrived.reshape(crop_count * group_count, local_modes, group_modes, C)

    def send_back(mixed_in):
        shaped = mixed_in.reshape(crop_count * group_count, local_modes, 1, group_modes, C)
        arrived = lax.all_to_all(shaped, "dp", split_axis=0, concat_axis=2, tiled=True)
        return jnp.transpose(arrived.reshape(crop_count, local_modes, MX, MZ, C), (0, 2, 1, 4, 3))

    owned = spectral_weight.reshape(local_modes, group_modes, C, C)
    coeffs = analyse(inputs)
    routed = send_out(coeffs)
    mixed_modes = send_back(bdot("bjgc,jgco->bjgo", routed, owned).astype(jnp.bfloat16))
    spectral = synthesise(mixed_modes)
    activation = bdot("bxycz,ch->bxyhz", inputs, w_in) + b_in[:, None]
    hidden = gelu_value(activation).astype(jnp.bfloat16)
    pre_gelu = bdot("bxyhz,hc->bxycz", hidden, w_out) + b_out[:, None] + spectral
    grad_pre = (cotangent.astype(jnp.float32) * gelu_slope(pre_gelu)).astype(jnp.bfloat16)
    grad_act = (bdot("bxycz,hc->bxyhz", grad_pre, w_out) * gelu_slope(activation)).astype(
        jnp.bfloat16
    )
    grad_coeffs = analyse(grad_pre)
    grad_routed = send_out(grad_coeffs)
    back_modes = send_back(bdot("bjgo,jgco->bjgc", grad_routed, owned).astype(jnp.bfloat16))
    grad_weight = (bdot("bjgc,bjgo->jgco", routed, grad_routed) * factor).reshape(
        local_modes, group_modes, C * C
    )
    grad_field = (bdot("bxyhz,ch->bxycz", grad_act, w_in) + synthesise(back_modes)).astype(
        jnp.bfloat16
    )
    return (grad_field, grad_weight)


def solution(mesh):
    return jax.shard_map(
        per_device,
        mesh=mesh,
        in_specs=(
            P("dp", "slab", None, None, None),
            P("dp", "slab", None, None, None),
            P("slab", "dp", None),
            P(),
            P(),
            P(),
            P(),
        ),
        out_specs=(P("dp", "slab", None, None, None), P("slab", "dp", None)),
        check_vma=False,
    )
```

profile of v0, /device:TPU:0, one launch (start us, length us, event | category | flops | bytes accessed | tf_op | source)
XLA Modules:
  0.0 158.9 jit_solution(14706031970246415845)
XLA Ops:
  1.0 1.5 copy-done
  2.5 2.5 %fusion.44 = bf16[8,24,64,16]{2,3,1,0:T(8,128)(2,1)S(1)} fusion(bf16[1,8,24,64,128]{4,3,2,1,0:T(8,128)(2,1)S(1)} %copy-done, bf16[8,128]{1,0:T(8,128)(2,1)S(1)} %get-tuple-element.7, bf16[8,128]{1,0:T(8,128)(2,1)S(1)} %get-tuple-element.6), kind=kOutput, calls=%fused_computation.45 | convolution fusion | flops 50536448 | bytes 3543040 | tf_op jit(solution)/shard_map/bxycz,kz->bxyck/dot_general | solution.py:43
  5.1 0.4 fusion.51
  5.4 0.9 copy.113
  6.4 2.1 %reshape.150 = bf16[4,2,16384]{2,1,0:T(2,128)(2,1)} reshape(bf16[16,1,8,16,64]{4,3,2,1,0:T(8,128)(2,1)} %bitcast.296) | data formatting | bytes 524288
  8.5 4.2 %all-to-all-start = ((bf16[4,2,16384]{2,1,0:T(2,128)(2,1)}), bf16[4,2,16384]{2,1,0:T(2,128)(2,1)S(1)}, u32[]{:S(2)}, u32[]{:S(2)}) async-start(bf16[4,2,16384]{2,1,0:T(2,128)(2,1)} %reshape.150), calls=%async_computation | async-start | bytes 524288 | tf_op jit(solution)/shard_map/all_to_all | solution.py:62
  12.9 5.9 %all-to-all-done = bf16[4,2,16384]{2,1,0:T(2,128)(2,1)S(1)} async-done(((bf16[4,2,16384]{2,1,0:T(2,128)(2,1)}), bf16[4,2,16384]{2,1,0:T(2,128)(2,1)S(1)}, u32[]{:S(2)}, u32[]{:S(2)}) %all-to-all-start) | async-done | bytes 262176 | tf_op jit(solution)/shard_map/all_to_all | solution.py:62
  18.8 1.2 reshape.151
  20.0 1.3 fusion.53
  21.3 0.9 reshape.152
  22.2 6.4 %all-to-all-start.1 = ((bf16[8,2,4096]{2,1,0:T(2,128)(2,1)}), bf16[8,2,4096]{2,1,0:T(2,128)(2,1)S(1)}, u32[]{:S(2)}, u32[]{:S(2)}) async-start(bf16[8,2,4096]{2,1,0:T(2,128)(2,1)} %reshape.152), calls=%async_computation.1 | async-start | bytes 262144 | tf_op jit(solution)/shard_map/all_to_all | solution.py:79
  28.6 4.2 %reshape.128 = bf16[4,32,64,64]{3,2,1,0:T(8,128)(2,1)} reshape(bf16[4,32,4096]{2,1,0:T(8,128)(2,1)} %param.9) | data formatting | bytes 2097152 | tf_op jit(solution)/shard_map/reshape | solution.py:87
  32.8 3.1 %all-to-all-done.1 = bf16[8,2,4096]{2,1,0:T(2,128)(2,1)S(1)} async-done(((bf16[8,2,4096]{2,1,0:T(2,128)(2,1)}), bf16[8,2,4096]{2,1,0:T(2,128)(2,1)S(1)}, u32[]{:S(2)}, u32[]{:S(2)}) %all-to-all-start.1) | async-done | bytes 131104 | tf_op jit(solution)/shard_map/all_to_all | solution.py:79
  36.2 2.2 %fusion.54 = bf16[8,4,1,32,64]{4,0,3,1,2:T(8,128)(2,1)S(1)} fusion(bf16[4,32,64,64]{3,2,1,0:T(8,128)(2,1)} %reshape.128, bf16[1,4,8,32,64]{4,3,1,0,2:T(8,128)(2,1)S(1)} %bitcast.289), kind=kOutput, calls=%fused_computation.61 | convolution fusion | flops 8454144 | bytes 1310720 | tf_op jit(solution)/shard_map/bjgc,jgco->bjgo/dot_general | solution.py:43
  38.4 0.8 copy.115
  39.2 1.9 %reshape.154 = bf16[8,2,4096]{2,1,0:T(2,128)(2,1)} reshape(bf16[8,1,4,32,64]{4,3,2,1,0:T(8,128)(2,1)} %bitcast.306) | data formatting | bytes 262144
  41.0 3.4 %all-to-all-start.2 = ((bf16[8,2,4096]{2,1,0:T(2,128)(2,1)}), bf16[8,2,4096]{2,1,0:T(2,128)(2,1)S(1)}, u32[]{:S(2)}, u32[]{:S(2)}) async-start(bf16[8,2,4096]{2,1,0:T(2,128)(2,1)} %reshape.154), calls=%async_computation.2 | async-start | bytes 262144 | tf_op jit(solution)/shard_map/all_to_all | solution.py:84
  44.4 10.9 %fusion.36 = f32[256,8,24,128]{3,0,2,1:T(8,128)} fusion(bf16[1,8,24,64,128]{4,3,2,1,0:T(8,128)(2,1)S(1)} %copy-done, bf16[64,256]{1,0:T(8,128)(2,1)} %param.10), kind=kOutput, calls=%fused_computation.38 | convolution fusion | flops 805306368 | bytes 28344320 | tf_op jit(solution)/shard_map/bxycz,ch->bxyhz/dot_general | solution.py:43
  55.5 0.3 fusion.49
  56.1 1.1 reshape.156
  57.2 3.6 %all-to-all-start.3 = ((bf16[4,2,16384]{2,1,0:T(2,128)(2,1)}), bf16[4,2,16384]{2,1,0:T(2,128)(2,1)S(1)}, u32[]{:S(2)}, u32[]{:S(2)}) async-start(bf16[4,2,16384]{2,1,0:T(2,128)(2,1)} %reshape.156), calls=%async_computation.3 | async-start | bytes 524288 | tf_op jit(solution)/shard_map/all_to_all | solution.py:70
  60.8 14.0 %fusion.11 = f32[8,24,128,64]{2,3,1,0:T(8,128)} fusion(f32[256,8,24,128]{3,0,2,1:T(8,128)} %fusion.36, f32[256]{0:T(256)} %param.11, bf16[256,64]{0,1:T(8,128)(2,1)} %param.12), kind=kOutput, calls=%fused_computation.15 | convolution fusion | flops 843055104 | bytes 31491072 | tf_op jit(solution)/shard_map/bxyhz,hc->bxycz/dot_general | solution.py:43
  74.8 0.3 reshape.157
  75.2 0.2 copy.41
  75.4 0.4 fusion.47
  75.8 6.9 %fusion.26 = bf16[1,8,24,64,128]{4,3,2,1,0:T(8,128)(2,1)S(1)} fusion(f32[8,24,128,64]{2,3,1,0:T(8,128)} %fusion.11, bf16[1,8,24,64,128]{4,3,2,1,0:T(8,128)(2,1)} %param.8, f32[64]{0:T(128)S(1)} %copy-done.11, bf16[8,24,64,16]{2,1,3,0:T(8,128)(2,1)S(1)} %fusion.47, bf16[8,128]{1,0:T(8,128)(2,1)S(1)} %copy-done.8, bf16[8,128]{1,0:T(8,128)(2,1)S(1)} %copy-done.6), kind=kOutput, calls=%fused_computation.27 | convolution fusion | flops 72359936 | bytes 12980480 | tf_op jit(solution)/shard_map/bxyck,kz->bxycz/dot_general | solution.py:43
  82.8 1.7 %copy-done.3 = bf16[1,8,24,64,128]{4,3,2,1,0:T(8,128)(2,1)} copy-done((bf16[1,8,24,64,128]{4,3,2,1,0:T(8,128)(2,1)}, bf16[1,8,24,64,128]{4,3,2,1,0:T(8,128)(2,1)S(1)}, u32[]{:S(2)}) %copy-start.3) | copy-done | bytes 3145752
  84.5 2.5 %fusion.41 = bf16[8,24,64,16]{2,3,1,0:T(8,128)(2,1)S(1)} fusion(bf16[1,8,24,64,128]{4,3,2,1,0:T(8,128)(2,1)S(1)} %fusion.26, bf16[8,128]{1,0:T(8,128)(2,1)S(1)} %copy-done.8, bf16[8,128]{1,0:T(8,128)(2,1)S(1)} %copy-done.6), kind=kOutput, calls=%fused_computation.44 | convolution fusion | flops 50536448 | bytes 3543040 | tf_op jit(solution)/shard_map/bxycz,kz->bxyck/dot_general | solution.py:43
  87.0 0.3 fusion.52
  87.5 0.4 reshape.158
  87.9 8.9 %all_to_all.120 = bf16[4,2,16384]{2,1,0:T(2,128)(2,1)S(1)} all-to-all(bf16[4,2,16384]{2,1,0:T(2,128)(2,1)S(1)} %reshape.158), channel_id=1, replica_groups=mesh['slab'=4,'dp'=8] {'slab'}, dimensions={0} | all-to-all | bytes 524288 | tf_op jit(solution)/shard_map/all_to_all | solution.py:62
  96.8 0.3 reshape.159
  97.2 0.2 fusion.55
  97.5 0.2 reshape.160
  97.7 13.1 %all_to_all.121 = bf16[8,2,4096]{2,1,0:T(2,128)(2,1)S(1)} all-to-all(bf16[8,2,4096]{2,1,0:T(2,128)(2,1)S(1)} %reshape.160), channel_id=1, replica_groups=mesh['slab'=4,'dp'=8] {'dp'}, dimensions={0} | all-to-all | bytes 262144 | tf_op jit(solution)/shard_map/all_to_all | solution.py:79
  111.0 1.2 fusion.56
  112.3 0.9 reshape.162
  113.1 3.6 %all-to-all-start.6 = ((bf16[8,2,4096]{2,1,0:T(2,128)(2,1)}), bf16[8,2,4096]{2,1,0:T(2,128)(2,1)S(1)}, u32[]{:S(2)}, u32[]{:S(2)}) async-start(bf16[8,2,4096]{2,1,0:T(2,128)(2,1)} %reshape.162), calls=%async_computation.6 | async-start | bytes 262144 | tf_op jit(solution)/shard_map/all_to_all | solution.py:84
  116.8 20.9 %fusion.13 = f32[8,24,128,64]{2,3,1,0:T(8,128)} fusion(f32[256,8,24,128]{3,0,2,1:T(8,128)} %fusion.36, f32[256]{0:T(256)S(1)} %copy-done.10, bf16[1,8,24,64,128]{4,3,2,1,0:T(8,128)(2,1)} %copy-done.3, bf16[256,64]{0,1:T(8,128)(2,1)S(1)} %copy-done.9, bf16[64,256]{1,0:T(8,128)(2,1)S(1)} %copy-done.4), kind=kOutput, calls=%fused_computation.16 | convolution fusion | flops 1679818752 | bytes 34669568 | tf_op jit(solution)/shard_map/bxyhz,ch->bxycz/dot_general | solution.py:43
  137.9 0.3 fusion.50
  138.4 1.1 reshape.164
  139.5 3.4 %all-to-all-start.7 = ((bf16[4,2,16384]{2,1,0:T(2,128)(2,1)}), bf16[4,2,16384]{2,1,0:T(2,128)(2,1)S(1)}, u32[]{:S(2)}, u32[]{:S(2)}) async-start(bf16[4,2,16384]{2,1,0:T(2,128)(2,1)} %reshape.164), calls=%async_computation.7 | async-start | bytes 524288 | tf_op jit(solution)/shard_map/all_to_all | solution.py:70
  143.0 2.7 %convolution_multiply_fusion = f32[4,32,64,64]{3,2,1,0:T(8,128)} fusion(bf16[1,4,8,32,64]{4,3,1,0,2:T(8,128)(2,1)S(1)} %bitcast.292, bf16[1,4,8,32,64]{4,3,1,0,2:T(8,128)(2,1)S(1)} %bitcast.290), kind=kOutput, calls=%fused_computation.40 | convolution fusion | flops 8912896 | bytes 2359296 | tf_op jit(solution)/shard_map/bjgc,bjgo->jgco/dot_general | solution.py:43
  145.7 4.8 %reshape.144 = f32[4,32,4096]{2,1,0:T(8,128)} reshape(f32[4,32,64,64]{3,2,1,0:T(8,128)} %convolution_multiply_fusion) | data formatting | bytes 4194304 | tf_op jit(solution)/shard_map/reshape | solution.py:102
  150.4 1.2 reshape.165
  151.6 1.4 copy.54
  153.0 0.4 fusion.48
  153.4 5.5 %fusion.27 = bf16[1,8,24,64,128]{4,3,2,1,0:T(8,128)(2,1)} fusion(f32[8,24,128,64]{2,3,1,0:T(8,128)} %fusion.13, bf16[8,24,64,16]{2,1,3,0:T(8,128)(2,1)S(1)} %fusion.48, bf16[8,128]{1,0:T(8,128)(2,1)S(1)} %copy-done.8, bf16[8,128]{1,0:T(8,128)(2,1)S(1)} %copy-done.6), kind=kOutput, calls=%fused_computation.29 | convolution fusion | flops 55058432 | bytes 9834496 | tf_op jit(solution)/shard_map/bxyck,kz->bxycz/dot_general | solution.py:43
  (49 shorter events, 2.2 us)
Async XLA Ops:
  0.6 1.9 %copy-start = (bf16[1,8,24,64,128]{4,3,2,1,0:T(8,128)(2,1)S(1)}, bf16[1,8,24,64,128]{4,3,2,1,0:T(8,128)(2,1)}, u32[]{:S(2)}) copy-start(bf16[1,8,24,64,128]{4,3,2,1,0:T(8,128)(2,1)} %param.7) | copy-start | bytes 9437188
  1.0 5.4 %copy-start.5 = (bf16[8,128]{1,0:T(8,128)(2,1)}, bf16[8,128]{1,0:T(8,128)(2,1)S(1)}, u32[]{:S(2)}) copy-start(bf16[8,128]{1,0:T(8,128)(2,1)S(1)} %get-tuple-element.6) | copy-start | bytes 6148
  1.0 5.4 %copy-start.7 = (bf16[8,128]{1,0:T(8,128)(2,1)}, bf16[8,128]{1,0:T(8,128)(2,1)S(1)}, u32[]{:S(2)}) copy-start(bf16[8,128]{1,0:T(8,128)(2,1)S(1)} %get-tuple-element.7) | copy-start | bytes 6148
  8.5 10.3 %all-to-all-start = ((bf16[4,2,16384]{2,1,0:T(2,128)(2,1)}), bf16[4,2,16384]{2,1,0:T(2,128)(2,1)S(1)}, u32[]{:S(2)}, u32[]{:S(2)}) async-start(bf16[4,2,16384]{2,1,0:T(2,128)(2,1)} %reshape.150), calls=%async_computation | async-start | bytes 524288 | tf_op jit(solution)/shard_map/all_to_all | solution.py:62
  22.2 13.7 %all-to-all-start.1 = ((bf16[8,2,4096]{2,1,0:T(2,128)(2,1)}), bf16[8,2,4096]{2,1,0:T(2,128)(2,1)S(1)}, u32[]{:S(2)}, u32[]{:S(2)}) async-start(bf16[8,2,4096]{2,1,0:T(2,128)(2,1)} %reshape.152), calls=%async_computation.1 | async-start | bytes 262144 | tf_op jit(solution)/shard_map/all_to_all | solution.py:79
  41.0 14.3 %all-to-all-start.2 = ((bf16[8,2,4096]{2,1,0:T(2,128)(2,1)}), bf16[8,2,4096]{2,1,0:T(2,128)(2,1)S(1)}, u32[]{:S(2)}, u32[]{:S(2)}) async-start(bf16[8,2,4096]{2,1,0:T(2,128)(2,1)} %reshape.154), calls=%async_computation.2 | async-start | bytes 262144 | tf_op jit(solution)/shard_map/all_to_all | solution.py:84
  57.2 17.6 %all-to-all-start.3 = ((bf16[4,2,16384]{2,1,0:T(2,128)(2,1)}), bf16[4,2,16384]{2,1,0:T(2,128)(2,1)S(1)}, u32[]{:S(2)}, u32[]{:S(2)}) async-start(bf16[4,2,16384]{2,1,0:T(2,128)(2,1)} %reshape.156), calls=%async_computation.3 | async-start | bytes 524288 | tf_op jit(solution)/shard_map/all_to_all | solution.py:70
  60.8 15.0 %copy-start.6 = (bf16[8,128]{1,0:T(8,128)(2,1)S(1)}, bf16[8,128]{1,0:T(8,128)(2,1)}, u32[]{:S(2)}) copy-start(bf16[8,128]{1,0:T(8,128)(2,1)} %copy-done.5) | copy-start | bytes 6148
  60.8 15.0 %copy-start.8 = (bf16[8,128]{1,0:T(8,128)(2,1)S(1)}, bf16[8,128]{1,0:T(8,128)(2,1)}, u32[]{:S(2)}) copy-start(bf16[8,128]{1,0:T(8,128)(2,1)} %copy-done.7) | copy-start | bytes 6148
  60.8 15.0 %copy-start.11 = (f32[64]{0:T(128)S(1)}, f32[64]{0:T(128)}, u32[]{:S(2)}) copy-start(f32[64]{0:T(128)} %param.13) | copy-start | bytes 772
  82.8 1.7 %copy-start.3 = (bf16[1,8,24,64,128]{4,3,2,1,0:T(8,128)(2,1)}, bf16[1,8,24,64,128]{4,3,2,1,0:T(8,128)(2,1)S(1)}, u32[]{:S(2)}) copy-start(bf16[1,8,24,64,128]{4,3,2,1,0:T(8,128)(2,1)S(1)} %fusion.26) | copy-start | bytes 9437188
  84.5 26.5 %copy-start.2 = (bf16[4,32,64,64]{3,2,1,0:T(8,128)(2,1)S(1)}, bf16[4,32,64,64]{3,2,1,0:T(8,128)(2,1)}, u32[]{:S(2)}) copy-start(bf16[4,32,64,64]{3,2,1,0:T(8,128)(2,1)} %reshape.128) | copy-start | bytes 3145732
  87.0 29.7 %copy-start.4 = (bf16[64,256]{1,0:T(8,128)(2,1)S(1)}, bf16[64,256]{1,0:T(8,128)(2,1)}, u32[]{:S(2)}) copy-start(bf16[64,256]{1,0:T(8,128)(2,1)} %param.10) | copy-start | bytes 98308
  87.0 29.8 %copy-start.9 = (bf16[256,64]{0,1:T(8,128)(2,1)S(1)}, bf16[256,64]{0,1:T(8,128)(2,1)}, u32[]{:S(2)}) copy-start(bf16[256,64]{0,1:T(8,128)(2,1)} %param.12) | copy-start | bytes 98308
  87.0 29.8 %copy-start.10 = (f32[256]{0:T(256)S(1)}, f32[256]{0:T(256)}, u32[]{:S(2)}) copy-start(f32[256]{0:T(256)} %param.11) | copy-start | bytes 3076
  113.1 24.5 %all-to-all-start.6 = ((bf16[8,2,4096]{2,1,0:T(2,128)(2,1)}), bf16[8,2,4096]{2,1,0:T(2,128)(2,1)S(1)}, u32[]{:S(2)}, u32[]{:S(2)}) async-start(bf16[8,2,4096]{2,1,0:T(2,128)(2,1)} %reshape.162), calls=%async_computation.6 | async-start | bytes 262144 | tf_op jit(solution)/shard_map/all_to_all | solution.py:84
  139.5 10.9 %all-to-all-start.7 = ((bf16[4,2,16384]{2,1,0:T(2,128)(2,1)}), bf16[4,2,16384]{2,1,0:T(2,128)(2,1)S(1)}, u32[]{:S(2)}, u32[]{:S(2)}) async-start(bf16[4,2,16384]{2,1,0:T(2,128)(2,1)} %reshape.164), calls=%async_computation.7 | async-start | bytes 524288 | tf_op jit(solution)/shard_map/all_to_all | solution.py:70
  151.6 7.3 %copy-start.1 = (bf16[1,8,24,64,128]{4,3,2,1,0:T(8,128)(2,1)S(1)}, bf16[1,8,24,64,128]{4,3,2,1,0:T(8,128)(2,1)}, u32[]{:S(2)}) copy-start(bf16[1,8,24,64,128]{4,3,2,1,0:T(8,128)(2,1)} %param.7) | copy-start | bytes 9437188
where the time goes:
time: 160 us; the launch traced here: 159 us
  matrix products  73.1 us (46%)
  local copies, waits for them, and re-layouts  28.8 us (18%)
  starting transfers between devices  24.6 us (15%)
  blocking collectives  21.9 us (14%)
  waiting for transfers between devices  9.02 us (6%)
    dot_general x18, matrix products, bdot(): return jnp.einsum(form, left, right, preferred_element_type=jnp.float32)  73.1 us
    unnamed x42, local copies, waits for them, and re-layouts  15.7 us
    all_to_all x1, blocking collectives, send_out(): lax.all_to_all(ordered, 'dp', split_axis=2, concat_axis=0, tiled=True)  13.1 us
    all_to_all x1, blocking collectives, analyse(): lax.all_to_all(along_y, 'slab', split_axis=2, concat_axis=1, tiled=True)  8.88 us
    all_to_all x2, starting transfers between devices, synthesise(): lax.all_to_all(back_x, 'slab', split_axis=1, concat_axis=2, tiled=True)  6.99 us
    all_to_all x2, starting transfers between devices, send_back(): lax.all_to_all(shaped, 'dp', split_axis=0, concat_axis=2, tiled=True)  6.96 us
    all_to_all x1, starting transfers between devices, send_out(): lax.all_to_all(ordered, 'dp', split_axis=2, concat_axis=0, tiled=True)  6.4 us
    all_to_all x1, waiting for transfers between devices, analyse(): lax.all_to_all(along_y, 'slab', split_axis=2, concat_axis=1, tiled=True)  5.9 us
  transfers between devices with their start and end apart: 6, of which 2 were waited for; matrix products, arithmetic and copies ran while one was open for 36% of the time, Pallas kernels for 0%

commit v1 on v0

--- a/solution.py
+++ b/solution.py
@@ -1,8 +1,13 @@
+import functools
 import math
 
 import jax
 import jax.numpy as jnp
+import ml_dtypes
+import numpy as np
 from jax import lax
+from jax.experimental import pallas as pl
+from jax.experimental.pallas import tpu as pltpu
 from jax.sharding import PartitionSpec as P
 
 C = 64
@@ -108,9 +113,346 @@
     return (grad_field, grad_weight)
 
 
+SLABS = 4
+GROUPS = 8
+XL = NX // SLABS
+JL = MY // SLABS
+GM = MX * MZ // GROUPS
+HID = 256
+UNITS = XL * NY // 4
+FACTOR = 8.0 / (NX * NY * NZ)
+F32 = jnp.float32
+BF16 = jnp.bfloat16
+STEP = 512
+
+
+def host_table(length, kept):
+    freq = np.concatenate([np.arange(kept // 2), np.arange(kept // 2) + 1])[:, None]
+    phase = (freq * np.arange(length)[None, :] % length).astype(np.float32)
+    phase = phase * np.float32(2.0 * math.pi / length)
+    return np.concatenate([np.cos(phase[: kept // 2]), np.sin(phase[kept // 2 :])], axis=0)
+
+
+def host_tables():
+    eye = np.eye(MZ, dtype=np.float32)
+    kz = np.kron(np.eye(8, dtype=np.float32), host_table(NZ, MZ))
+    ky = np.kron(host_table(NY, MY), eye)
+    kx = np.kron(host_table(NX, MX), eye)
+    spread = np.repeat(np.eye(C, dtype=np.float32), C, axis=1)
+    tables = (kz, kz.T, ky, ky.T, kx, kx.T, spread, spread.T)
+    return tuple(jnp.asarray(np.ascontiguousarray(t).astype(ml_dtypes.bfloat16)) for t in tables)
+
+
+def dot(left, right):
+    return jnp.dot(left, right, preferred_element_type=F32)
+
+
+def fused_kernel(
+    x_hbm, ct_hbm, w_hbm, w_in, w_in_t, b_in, w_out, w_out_t, b_out,
+    kz, kz_t, ky, ky_t, kx, kx_t, spread, spread_t,
+    gx_hbm, gw_hbm,
+    x_v, ct_v, w_v, gw_v, slope_v, part_v, gp_v, along_z, rows_v,
+    send_s, recv_s, send_g, recv_g, send_sem, recv_sem, load_sem, store_sem,
+):
+    slab = lax.axis_index("slab")
+    group = lax.axis_index("dp")
+
+    loads = [
+        pltpu.make_async_copy(x_hbm, x_v, load_sem.at[0]),
+        pltpu.make_async_copy(ct_hbm, ct_v, load_sem.at[1]),
+        pltpu.make_async_copy(w_hbm, w_v, load_sem.at[2]),
+    ]
+    for load in loads:
+        load.start()
+
+    barrier = pltpu.get_barrier_semaphore()
+    for r in range(1, SLABS):
+        pl.semaphore_signal(
+            barrier, inc=1, device_id={"slab": lax.rem(slab + r, SLABS)},
+            device_id_type=pl.DeviceIdType.MESH,
+        )
+    for r in range(1, GROUPS):
+        pl.semaphore_signal(
+            barrier, inc=1, device_id={"dp": lax.rem(group + r, GROUPS)},
+            device_id_type=pl.DeviceIdType.MESH,
+        )
+
+    def exchange(phase, send, recv, axis, me, count):
+        copies = []
+        for r in range(1, count):
+            dest = lax.rem(me + r, count)
+            copy = pltpu.make_async_remote_copy(
+                src_ref=send.at[dest],
+                dst_ref=recv.at[me],
+                send_sem=send_sem.at[phase, r - 1],
+                recv_sem=recv_sem.at[phase, r - 1],
+                device_id={axis: dest},
+                device_id_type=pl.DeviceIdType.MESH,
+            )
+            copy.start()
+            copies.append(copy)
+        recv[me] = send[me]
+        return copies
+
+    def finish(copies):
+        for copy in copies:
+            copy.wait()
+
+    def over_slabs(phase):
+        return exchange(phase, send_s.at[phase // 2], recv_s.at[phase // 2], "slab", slab, SLABS)
+
+    def over_groups(phase):
+        return exchange(phase, send_g.at[phase // 2], recv_g.at[phase // 2], "dp", group, GROUPS)
+
+    def lanes_of(ref, plane, first, count):
+        return jnp.concatenate([ref[plane * NY + first + q] for q in range(count)], axis=1)
+
+    def send_along_y(phase):
+        along_y = dot(along_z[...], ky_t[...])
+        for xl in range(XL):
+            turned = along_y[xl * C : (xl + 1) * C].T
+            for s in range(SLABS):
+                for p in range(JL // 2):
+                    j = s * JL + 2 * p
+                    pair = jnp.concatenate(
+                        [turned[j * MZ : (j + 1) * MZ], turned[(j + 1) * MZ : (j + 2) * MZ]], axis=1
+                    )
+                    send_s[phase // 2, s, xl * MZ : (xl + 1) * MZ, 2 * p * C : 2 * (p + 1) * C] = (
+                        pair.astype(BF16)
+                    )
+        return over_slabs(phase)
+
+    def send_modes(phase):
+        arrived = recv_s[(phase - 1) // 2].reshape(NX * MZ, JL * C)
+        modes = dot(kx[...], arrived).astype(BF16)
+        send_g[phase // 2] = modes.reshape(GROUPS, GM, JL * C)
+        return over_groups(phase)
+
+    def send_planes(phase):
+        arrived = recv_g[(phase - 1) // 2].reshape(MX * MZ, JL * C)
+        planes = dot(kx_t[...], arrived).astype(BF16)
+        send_s[phase // 2] = planes.reshape(SLABS, XL * MZ, JL * C)
+        return over_slabs(phase)
+
+    def back_along_y(phase):
+        for xl in range(XL):
+            blocks = []
+            for s in range(SLABS):
+                rows = recv_s[phase // 2, s, xl * MZ : (xl + 1) * MZ, :].astype(F32)
+                for jl in range(JL):
+                    blocks.append(rows[:, jl * C : (jl + 1) * C])
+            turned = jnp.concatenate(blocks, axis=0).T
+            rows_v[xl * C : (xl + 1) * C, :] = turned.astype(BF16)
+        along_z[...] = dot(rows_v[...], ky[...]).astype(BF16)
+
+    def plane_rows(xl):
+        return pl.ds(pl.multiple_of(xl * C, C), C)
+
+    def forward_units(first, last):
+        def unit(u, carry):
+            plane, part = u // (NY // 4), lax.rem(u, NY // 4)
+            samples = lanes_of(x_v, plane, part * 4, 4)
+            act = dot(w_in_t[...], samples) + b_in[...]
+            phi = 0.5 + 0.5 * lax.erf(act * root_half)
+            bell = jnp.exp(act * act * -0.5) * inv_root_two_pi
+            slope_v[u] = (phi + act * bell).astype(BF16)
+            part_v[u] = dot(w_out_t[...], (act * phi).astype(BF16)) + b_out[...]
+            return carry
+
+        lax.fori_loop(first, last, unit, 0)
+
+    def backward_units(first, last):
+        def unit(u, carry):
+            grad = dot(w_out[...], gp_v[u]) * slope_v[u].astype(F32)
+            part_v[u] = dot(w_in[...], grad.astype(BF16))
+            return carry
+
+        lax.fori_loop(first, last, unit, 0)
+
+    loads[0].wait()
+
+    def analyse_plane(xl, carry):
+        for t in range(NY // 8):
+            samples = lanes_of(x_v, xl, t * 8, 8)
+            along_z[plane_rows(xl), t * 128 : (t + 1) * 128] = dot(samples, kz_t[...]).astype(BF16)
+        return carry
+
+    lax.fori_loop(0, XL, analyse_plane, 0)
+    pl.semaphore_wait(barrier, SLABS + GROUPS - 2)
+    flight = send_along_y(0)
+    forward_units(0, 12)
+    finish(flight)
+    flight = send_modes(1)
+    forward_units(12, 24)
+    finish(flight)
+
+    loads[2].wait()
+    coeffs = recv_g.at[0]
+    grads = recv_g.at[2]
+
+    def pair_rows(ref, p):
+        return ref[:, :, 2 * p * C : 2 * (p + 1) * C].reshape(GROUPS * GM, 2 * C)
+
+    for p in range(JL // 2):
+        pair = pair_rows(coeffs, p)
+        mixed = []
+        for half in range(2):
+            jl = 2 * p + half
+            rows = pair[:, half * C : (half + 1) * C]
+
+            def mix(n, total, rows=rows, jl=jl):
+                span = pl.ds(pl.multiple_of(n * STEP, STEP), STEP)
+                wide = dot(rows, spread[:, span]).reshape(GROUPS, GM, STEP)
+                term = (wide * w_v[jl, :, span].astype(F32)[None]).reshape(GROUPS * GM, STEP)
+                return total + sum(term[:, q * 128 : (q + 1) * 128] for q in range(STEP // 128))
+
+            total = lax.fori_loop(0, C * C // STEP, mix, jnp.zeros((GROUPS * GM, 2 * C), F32))
+            mixed.append(total[:, :C] + total[:, C:])
+        send_g[1, :, :, 2 * p * C : 2 * (p + 1) * C] = (
+            jnp.concatenate(mixed, axis=1).astype(BF16).reshape(GROUPS, GM, 2 * C)
+        )
+    flight = over_groups(2)
+    forward_units(24, 36)
+    finish(flight)
+    flight = send_planes(3)
+    forward_units(36, UNITS)
+    finish(flight)
+    back_along_y(3)
+
+    loads[1].wait()
+
+    def middle_plane(xl, carry):
+        for t in range(NY // 8):
+            kept = along_z[plane_rows(xl), t * 128 : (t + 1) * 128]
+            u = xl * (NY // 4) + 2 * t
+            pre = jnp.concatenate([part_v[u], part_v[u + 1]], axis=1) + dot(kept, kz[...]) * FACTOR
+            phi = 0.5 + 0.5 * lax.erf(pre * root_half)
+            slope = phi + pre * jnp.exp(pre * pre * -0.5) * inv_root_two_pi
+            grad = (lanes_of(ct_v, xl, t * 8, 8).astype(F32) * slope).astype(BF16)
+            gp_v[u] = grad[:, :512]
+            gp_v[u + 1] = grad[:, 512:]
+            along_z[plane_rows(xl), t * 128 : (t + 1) * 128] = dot(grad, kz_t[...]).astype(BF16)
+        return carry
+
+    lax.fori_loop(0, XL, middle_plane, 0)
+    flight = send_along_y(4)
+    backward_units(0, 16)
+    finish(flight)
+    flight = send_modes(5)
+    backward_units(16, 32)
+    finish(flight)
+
+    for p in range(JL // 2):
+        pair = pair_rows(grads, p).astype(F32)
+        mixed = []
+        for half in range(2):
+            jl = 2 * p + half
+            rows = pair[:, half * C : (half + 1) * C]
+            twice = jnp.concatenate([rows, rows], axis=1)
+            wide = jnp.concatenate([twice] * (STEP // 128), axis=1).reshape(GROUPS, GM, STEP)
+
+            def mix_back(n, total, wide=wide, jl=jl):
+                span = pl.ds(pl.multiple_of(n * STEP, STEP), STEP)
+                term = wide * w_v[jl, :, span].astype(F32)[None]
+                return total + dot(term.astype(BF16).reshape(GROUPS * GM, STEP), spread_t[span, :])
+
+            mixed.append(
+                lax.fori_loop(0, C * C // STEP, mix_back, jnp.zeros((GROUPS * GM, C), F32))
+            )
+        send_g[3, :, :, 2 * p * C : 2 * (p + 1) * C] = (
+            jnp.concatenate(mixed, axis=1).astype(BF16).reshape(GROUPS, GM, 2 * C)
+        )
+    flight = over_groups(6)
+
+    for p in range(JL // 2):
+        pair = pair_rows(coeffs, p)
+        grad_pair = pair_rows(grads, p).astype(F32)
+        for half in range(2):
+            jl = 2 * p + half
+            rows = pair[:, half * C : (half + 1) * C]
+            grad_rows = grad_pair[:, half * C : (half + 1) * C] * FACTOR
+            twice = jnp.concatenate([grad_rows, grad_rows], axis=1)
+            wide = jnp.concatenate([twice] * (STEP // 128), axis=1)
+
+            def outer(n, carry, rows=rows, wide=wide, jl=jl):
+                span = pl.ds(pl.multiple_of(n * STEP, STEP), STEP)
+                term = (dot(rows, spread[:, span]) * wide).reshape(GROUPS, GM, STEP)
+                gw_v[jl, :, span] = jnp.sum(term, axis=0)
+                return carry
+
+            lax.fori_loop(0, C * C // STEP, outer, 0)
+    store_gw = pltpu.make_async_copy(gw_v, gw_hbm, store_sem.at[0])
+    store_gw.start()
+    finish(flight)
+    flight = send_planes(7)
+    backward_units(32, UNITS)
+    finish(flight)
+    back_along_y(7)
+
+    def last_plane(xl, carry):
+        for t in range(NY // 8):
+            kept = along_z[plane_rows(xl), t * 128 : (t + 1) * 128]
+            u = xl * (NY // 4) + 2 * t
+            total = jnp.concatenate([part_v[u], part_v[u + 1]], axis=1)
+            total = (total + dot(kept, kz[...]) * FACTOR).astype(BF16)
+            for q in range(8):
+                ct_v[xl * NY + t * 8 + q] = total[:, q * NZ : (q + 1) * NZ]
+        return carry
+
+    lax.fori_loop(0, XL, last_plane, 0)
+    store_gx = pltpu.make_async_copy(ct_v, gx_hbm, store_sem.at[1])
+    store_gx.start()
+    store_gw.wait()
+    store_gx.wait()
+
+
+def fused_device(inputs, cotangent, spectral_weight, w_in, b_in, w_out, b_out):
+    field = inputs.shape
+    flat = (XL * NY, C, NZ)
+    any_spec = pl.BlockSpec(memory_space=pl.ANY)
+    vmem_spec = pl.BlockSpec(memory_space=pltpu.VMEM)
+    out = pl.pallas_call(
+        fused_kernel,
+        out_shape=(
+            jax.ShapeDtypeStruct(flat, BF16),
+            jax.ShapeDtypeStruct((JL, GM, C * C), F32),
+        ),
+        in_specs=[any_spec] * 3 + [vmem_spec] * 14,
+        out_specs=(any_spec, any_spec),
+        scratch_shapes=[
+            pltpu.VMEM(flat, BF16),
+            pltpu.VMEM(flat, BF16),
+            pltpu.VMEM((JL, GM, C * C), BF16),
+            pltpu.VMEM((JL, GM, C * C), F32),
+            pltpu.VMEM((UNITS, HID, 4 * NZ), BF16),
+            pltpu.VMEM((UNITS, C, 4 * NZ), F32),
+            pltpu.VMEM((UNITS, C, 4 * NZ), BF16),
+            pltpu.VMEM((XL * C, NY * MZ), BF16),
+            pltpu.VMEM((XL * C, MY * MZ), BF16),
+            pltpu.VMEM((4, SLABS, XL * MZ, JL * C), BF16),
+            pltpu.VMEM((4, SLABS, XL * MZ, JL * C), BF16),
+            pltpu.VMEM((4, GROUPS, GM, JL * C), BF16),
+            pltpu.VMEM((4, GROUPS, GM, JL * C), BF16),
+            pltpu.SemaphoreType.DMA((8, GROUPS - 1)),
+            pltpu.SemaphoreType.DMA((8, GROUPS - 1)),
+            pltpu.SemaphoreType.DMA((3,)),
+            pltpu.SemaphoreType.DMA((2,)),
+        ],
+        compiler_params=pltpu.CompilerParams(
+            collective_id=0, has_side_effects=True, vmem_limit_bytes=60 * 1024 * 1024
+        ),
+    )(
+        inputs.reshape(flat), cotangent.reshape(flat), spectral_weight,
+        w_in, w_in.T, b_in[:, None], w_out, w_out.T, b_out[:, None], *host_tables(),
+    )
+    return out[0].reshape(field), out[1]
+
+
 def solution(mesh):
+    sizes = (mesh.shape["slab"], mesh.shape["dp"])
+    body = fused_device if sizes == (SLABS, GROUPS) else per_device
     return jax.shard_map(
-        per_device,
+        body,
         mesh=mesh,
         in_specs=(
             P("dp", "slab", None, None, None),

time: 160 us -> 102 us (0.64)
  Pallas kernels: 0 us -> 89.5 us
  matrix products: 73.1 us -> 0 us
  starting transfers between devices: 24.6 us -> 0 us
  blocking collectives: 21.9 us -> 0 us
  local copies, waits for them, and re-layouts: 28.8 us -> 11.7 us
  waiting for transfers between devices: 9.02 us -> 0 us
    pallas_call x0 -> x1, Pallas kernels: none -> 89.5 us  [fused_device(): pl.pallas_call(fused_kernel, out_shape=(jax.ShapeDtypeStruct(flat, BF16),...]
    dot_general x18 -> x0, matrix products: 73.1 us -> none  [bdot(): return jnp.einsum(form, left, right, preferred_element_type=jnp.float32)]
    all_to_all x6 -> x0, starting transfers between devices: 24.6 us -> none  [the longest x2 6.99 us: synthesise(): lax.all_to_all(back_x, 'slab', split_axis=1, concat_axis=2, tiled=True)]
    all_to_all x2 -> x0, blocking collectives: 21.9 us -> none  [the longest x1 13.1 us: send_out(): lax.all_to_all(ordered, 'dp', split_axis=2, concat_axis=0, tiled=True)]
    reshape x4 -> x0, local copies, waits for them, and re-layouts: 9.81 us -> none  [the longest x1 4.76 us: per_device(): (bdot('bjgc,bjgo->jgco', routed, grad_routed) * factor).reshape(local_mod...]
    all_to_all x6 -> x0, waiting for transfers between devices: 9.02 us -> none  [the longest x1 5.9 us: analyse(): lax.all_to_all(along_y, 'slab', split_axis=2, concat_axis=1, tiled=True)]
    unnamed x42 -> x6, local copies, waits for them, and re-layouts: 15.7 us -> 8.89 us
    broadcast_in_dim x0 -> x2, local copies, waits for them, and re-layouts: none -> 2.82 us  [the longest x1 1.47 us: fused_device(): b_in[:, None]]
  transfers between devices with their start and end apart: 6 -> 0, of which waited for: 2 -> 0; matrix products, arithmetic and copies ran while one was open for 36% -> 0% of each run, Pallas kernels for 0% -> 0%
where the time goes in v1:
time: 102 us
  Pallas kernels  89.5 us (88%)
  local copies, waits for them, and re-layouts  11.7 us (11%)
    pallas_call x1, Pallas kernels, fused_device(): pl.pallas_call(fused_kernel, out_shape=(jax.ShapeDtypeStruct(flat, BF16),...  89.5 us
    unnamed x6, local copies, waits for them, and re-layouts  8.89 us

profile of v1, /device:TPU:0, one launch (start us, length us, event | category | flops | bytes accessed | tf_op | source)
XLA Modules:
  0.0 101.9 jit_solution(1406422236586920095)
XLA Ops:
  0.6 1.3 %copy.23.b_out = f32[64,1]{1,0:T(8,128)} copy(f32[64,1]{0,1:T(1,128)} %bitcast.13) | data formatting | bytes 512 | tf_op jit(solution)/shard_map/broadcast_in_dim | solution.py:446
  2.0 1.5 %copy.20 = bf16[64,256]{0,1:T(8,128)(2,1)} copy(bf16[64,256]{1,0:T(8,128)(2,1)} %w_in.1) | data formatting | bytes 65536 | tf_op args[3]
  3.5 1.5 %copy.22.w_out = bf16[256,64]{1,0:T(8,128)(2,1)} copy(bf16[256,64]{0,1:T(8,128)(2,1)} %param.20) | data formatting | bytes 65536 | tf_op args[5]
  5.0 1.5 %copy.21.b_in = f32[256,1]{1,0:T(8,128)} copy(f32[256,1]{0,1:T(1,128)} %bitcast.12) | data formatting | bytes 2048 | tf_op jit(solution)/shard_map/broadcast_in_dim | solution.py:446
  6.4 89.5 %shard_map.158 = (bf16[192,64,128]{2,1,0:T(8,128)(2,1)}, f32[4,32,4096]{2,1,0:T(8,128)}) custom-call(bf16[192,64,128]{2,1,0:T(8,128)(2,1)} %bitcast.8, bf16[192,64,128]{2,1,0:T(8,128)(2,1)} %bitcast.9, bf16[4,32,4096]{2,1,0:T(8,128)(2,1)} %w_hbm.1, bf16[64,256]{1,0:T(8,128)(2,1)} %w_in.1, bf16[256,64]{1,0:T(8,128)(2,1)} %bitcast.10, f32[256,1]{1,0:T(8,128)} %copy.21.b_in, ...), custom_call_target="tpu_custom_call" | custom-call | tf_op jit(solution)/shard_map/pallas_call | solution.py:414
  95.9 0.0 copy-start
  95.9 4.6 %copy.26 = bf16[1,8,24,64,128]{4,3,2,1,0:T(8,128)(2,1)} copy(bf16[1,8,24,64,128]{4,3,2,1,0:T(8,128)(2,1)} %bitcast.7) | data formatting | bytes 6291456
  100.5 0.0 copy-done
  100.5 1.3 %copy.27 = f32[4,32,4096]{2,1,0:T(8,128)} copy(f32[4,32,4096]{2,1,0:T(8,128)S(1)} %copy-done) | data formatting | bytes 4194304
Async XLA Ops:
  95.9 4.6 %copy-start = (f32[4,32,4096]{2,1,0:T(8,128)S(1)}, f32[4,32,4096]{2,1,0:T(8,128)}, u32[]{:S(2)}) copy-start(f32[4,32,4096]{2,1,0:T(8,128)} %get-tuple-element.9) | copy-start | bytes 6291460

commit v2 on v1

--- a/solution.py
+++ b/solution.py
@@ -124,6 +124,7 @@
 F32 = jnp.float32
 BF16 = jnp.bfloat16
 STEP = 512
+HALF_LOG2_E = 0.5 / math.log(2.0)
 
 
 def host_table(length, kept):
@@ -148,11 +149,12 @@
 
 
 def fused_kernel(
-    x_hbm, ct_hbm, w_hbm, w_in, w_in_t, b_in, w_out, w_out_t, b_out,
+    x_hbm, ct_hbm, w_hbm, w_in, b_in, w_out_t, b_out,
     kz, kz_t, ky, ky_t, kx, kx_t, spread, spread_t,
     gx_hbm, gw_hbm,
     x_v, ct_v, w_v, gw_v, slope_v, part_v, gp_v, along_z, rows_v,
-    send_s, recv_s, send_g, recv_g, send_sem, recv_sem, load_sem, store_sem,
+    send_s, recv_s, send_g, recv_g, wide_v, first_v, w_out, bias_v,
+    send_sem, recv_sem, load_sem, store_sem,
 ):
     slab = lax.axis_index("slab")
     group = lax.axis_index("dp")
@@ -176,6 +178,16 @@
             barrier, inc=1, device_id={"dp": lax.rem(group + r, GROUPS)},
             device_id_type=pl.DeviceIdType.MESH,
         )
+
+    bias = b_in[...]
+    high = bias.astype(BF16).astype(F32)
+    middle = (bias - high).astype(BF16).astype(F32)
+    low = bias - high - middle
+    row = lax.broadcasted_iota(jnp.int32, (C, HID), 0)
+    bias_rows = jnp.where(row == 0, high, jnp.where(row == 1, middle, jnp.where(row == 2, low, 0.0)))
+    first_v[...] = jnp.concatenate([w_in[...].astype(F32), bias_rows], axis=0).T.astype(BF16)
+    w_out[...] = w_out_t[...].astype(F32).T.astype(BF16)
+    bias_v[...] = jnp.broadcast_to(b_out[...], (128, C)).T
 
     def exchange(phase, send, recv, axis, me, count):
         copies = []
@@ -252,22 +264,23 @@
         def unit(u, carry):
             plane, part = u // (NY // 4), lax.rem(u, NY // 4)
             samples = lanes_of(x_v, plane, part * 4, 4)
-            act = dot(w_in_t[...], samples) + b_in[...]
-            phi = 0.5 + 0.5 * lax.erf(act * root_half)
-            bell = jnp.exp(act * act * -0.5) * inv_root_two_pi
-            slope_v[u] = (phi + act * bell).astype(BF16)
-            part_v[u] = dot(w_out_t[...], (act * phi).astype(BF16)) + b_out[...]
+            ones = jnp.ones((16, 4 * NZ), BF16)
+            act = dot(first_v[:, : C + 16], jnp.concatenate([samples, ones], axis=0)).astype(BF16)
+            phi = lax.erf(act * root_half) * 0.5 + 0.5
+            bell = jnp.exp2(act * act * -HALF_LOG2_E) * inv_root_two_pi
+            slope_v[u] = phi + act * bell
+            part_v[u] = dot(w_out_t[...], act * phi) + jnp.concatenate([bias_v[...]] * 4, axis=1)
             return carry
 
-        lax.fori_loop(first, last, unit, 0)
+        lax.fori_loop(first, last, unit, 0, unroll=2)
 
     def backward_units(first, last):
         def unit(u, carry):
-            grad = dot(w_out[...], gp_v[u]) * slope_v[u].astype(F32)
-            part_v[u] = dot(w_in[...], grad.astype(BF16))
+            grad = dot(w_out[...], gp_v[u]).astype(BF16) * slope_v[u]
+            part_v[u] = dot(w_in[...], grad)
             return carry
 
-        lax.fori_loop(first, last, unit, 0)
+        lax.fori_loop(first, last, unit, 0, unroll=4)
 
     loads[0].wait()
 
@@ -302,11 +315,14 @@
 
             def mix(n, total, rows=rows, jl=jl):
                 span = pl.ds(pl.multiple_of(n * STEP, STEP), STEP)
-                wide = dot(rows, spread[:, span]).reshape(GROUPS, GM, STEP)
-                term = (wide * w_v[jl, :, span].astype(F32)[None]).reshape(GROUPS * GM, STEP)
+                wide = dot(rows, spread[:, span])
+                wide_v[jl, :, span] = wide.astype(BF16)
+                term = (wide.reshape(GROUPS, GM, STEP) * w_v[jl, :, span].astype(F32)[None]).reshape(GROUPS * GM, STEP)
                 return total + sum(term[:, q * 128 : (q + 1) * 128] for q in range(STEP // 128))
 
-            total = lax.fori_loop(0, C * C // STEP, mix, jnp.zeros((GROUPS * GM, 2 * C), F32))
+            total = lax.fori_loop(
+                0, C * C // STEP, mix, jnp.zeros((GROUPS * GM, 2 * C), F32), unroll=4
+            )
             mixed.append(total[:, :C] + total[:, C:])
         send_g[1, :, :, 2 * p * C : 2 * (p + 1) * C] = (
             jnp.concatenate(mixed, axis=1).astype(BF16).reshape(GROUPS, GM, 2 * C)
@@ -343,7 +359,7 @@
     finish(flight)
 
     for p in range(JL // 2):
-        pair = pair_rows(grads, p).astype(F32)
+        pair = pair_rows(grads, p)
         mixed = []
         for half in range(2):
             jl = 2 * p + half
@@ -353,11 +369,13 @@
 
             def mix_back(n, total, wide=wide, jl=jl):
                 span = pl.ds(pl.multiple_of(n * STEP, STEP), STEP)
-                term = wide * w_v[jl, :, span].astype(F32)[None]
-                return total + dot(term.astype(BF16).reshape(GROUPS * GM, STEP), spread_t[span, :])
+                term = wide * w_v[jl, :, span][None]
+                return total + dot(term.reshape(GROUPS * GM, STEP), spread_t[span, :])
 
             mixed.append(
-                lax.fori_loop(0, C * C // STEP, mix_back, jnp.zeros((GROUPS * GM, C), F32))
+                lax.fori_loop(
+                    0, C * C // STEP, mix_back, jnp.zeros((GROUPS * GM, C), F32), unroll=4
+                )
             )
         send_g[3, :, :, 2 * p * C : 2 * (p + 1) * C] = (
             jnp.concatenate(mixed, axis=1).astype(BF16).reshape(GROUPS, GM, 2 * C)
@@ -365,22 +383,19 @@
     flight = over_groups(6)
 
     for p in range(JL // 2):
-        pair = pair_rows(coeffs, p)
         grad_pair = pair_rows(grads, p).astype(F32)
         for half in range(2):
             jl = 2 * p + half
-            rows = pair[:, half * C : (half + 1) * C]
             grad_rows = grad_pair[:, half * C : (half + 1) * C] * FACTOR
-            twice = jnp.concatenate([grad_rows, grad_rows], axis=1)
-            wide = jnp.concatenate([twice] * (STEP // 128), axis=1)
-
-            def outer(n, carry, rows=rows, wide=wide, jl=jl):
-                span = pl.ds(pl.multiple_of(n * STEP, STEP), STEP)
-                term = (dot(rows, spread[:, span]) * wide).reshape(GROUPS, GM, STEP)
-                gw_v[jl, :, span] = jnp.sum(term, axis=0)
+            wide = jnp.concatenate([grad_rows, grad_rows], axis=1).reshape(GROUPS, GM, 2 * C)
+
+            def outer(n, carry, wide=wide, jl=jl):
+                span = pl.ds(pl.multiple_of(n * 128, 128), 128)
+                left = wide_v[jl, :, span].astype(F32).reshape(GROUPS, GM, 2 * C)
+                gw_v[jl, :, span] = jnp.sum(left * wide, axis=0)
                 return carry
 
-            lax.fori_loop(0, C * C // STEP, outer, 0)
+            lax.fori_loop(0, C * C // 128, outer, 0, unroll=4)
     store_gw = pltpu.make_async_copy(gw_v, gw_hbm, store_sem.at[0])
     store_gw.start()
     finish(flight)
@@ -417,7 +432,7 @@
             jax.ShapeDtypeStruct(flat, BF16),
             jax.ShapeDtypeStruct((JL, GM, C * C), F32),
         ),
-        in_specs=[any_spec] * 3 + [vmem_spec] * 14,
+        in_specs=[any_spec] * 3 + [vmem_spec] * 12,
         out_specs=(any_spec, any_spec),
         scratch_shapes=[
             pltpu.VMEM(flat, BF16),
@@ -433,6 +448,10 @@
             pltpu.VMEM((4, SLABS, XL * MZ, JL * C), BF16),
             pltpu.VMEM((4, GROUPS, GM, JL * C), BF16),
             pltpu.VMEM((4, GROUPS, GM, JL * C), BF16),
+            pltpu.VMEM((JL, GROUPS * GM, C * C), BF16),
+            pltpu.VMEM((HID, 2 * C), BF16),
+            pltpu.VMEM((HID, C), BF16),
+            pltpu.VMEM((C, 128), F32),
             pltpu.SemaphoreType.DMA((8, GROUPS - 1)),
             pltpu.SemaphoreType.DMA((8, GROUPS - 1)),
             pltpu.SemaphoreType.DMA((3,)),
@@ -443,7 +462,7 @@
         ),
     )(
         inputs.reshape(flat), cotangent.reshape(flat), spectral_weight,
-        w_in, w_in.T, b_in[:, None], w_out, w_out.T, b_out[:, None], *host_tables(),
+        w_in, b_in[None], w_out.T, b_out[None], *host_tables(),
     )
     return out[0].reshape(field), out[1]
 

time: 102 us -> 75.4 us (0.74)
  Pallas kernels: 89.5 us -> 68.7 us
  local copies, waits for them, and re-layouts: 11.7 us -> 5.92 us
    pallas_call x1, Pallas kernels: 89.5 us -> 68.7 us  [fused_device(): pl.pallas_call(fused_kernel, out_shape=(jax.ShapeDtypeStruct(flat, BF16),...]
    unnamed x6 -> x4, local copies, waits for them, and re-layouts: 8.89 us -> 5.92 us
    broadcast_in_dim x2 -> x0, local copies, waits for them, and re-layouts: 2.82 us -> none  [the longest x1 1.47 us: fused_device(): b_in[:, None]]
where the time goes in v2:
time: 75.4 us; the launch traced here: 75.3 us
  Pallas kernels  68.7 us (91%)
  local copies, waits for them, and re-layouts  5.92 us (8%)
    pallas_call x1, Pallas kernels, fused_device(): pl.pallas_call(fused_kernel, out_shape=(jax.ShapeDtypeStruct(flat, BF16),...  68.7 us
    unnamed x4, local copies, waits for them, and re-layouts  5.92 us

profile of v2, /device:TPU:0, one launch (start us, length us, event | category | flops | bytes accessed | tf_op | source)
XLA Modules:
  0.0 75.3 jit_solution(3471744734998227533)
XLA Ops:
  0.6 68.7 %shard_map.158 = (bf16[192,64,128]{2,1,0:T(8,128)(2,1)}, f32[4,32,4096]{2,1,0:T(8,128)}) custom-call(bf16[192,64,128]{2,1,0:T(8,128)(2,1)} %bitcast.7, bf16[192,64,128]{2,1,0:T(8,128)(2,1)} %bitcast.8, bf16[4,32,4096]{2,1,0:T(8,128)(2,1)} %w_hbm.1, bf16[64,256]{1,0:T(8,128)(2,1)} %w_in.1, f32[1,256]{1,0:T(1,128)} %bitcast.10, bf16[64,256]{1,0:T(8,128)(2,1)} %bitcast.9, ...), custom_call_target="tpu_custom_call" | custom-call | tf_op jit(solution)/shard_map/pallas_call | solution.py:429
  69.4 0.0 copy-start
  69.4 4.6 %copy.19 = bf16[1,8,24,64,128]{4,3,2,1,0:T(8,128)(2,1)} copy(bf16[1,8,24,64,128]{4,3,2,1,0:T(8,128)(2,1)} %bitcast.6) | data formatting | bytes 6291456
  74.0 0.0 copy-done
  74.0 1.3 %copy.20 = f32[4,32,4096]{2,1,0:T(8,128)} copy(f32[4,32,4096]{2,1,0:T(8,128)S(1)} %copy-done) | data formatting | bytes 4194304
Async XLA Ops:
  69.4 4.6 %copy-start = (f32[4,32,4096]{2,1,0:T(8,128)S(1)}, f32[4,32,4096]{2,1,0:T(8,128)}, u32[]{:S(2)}) copy-start(f32[4,32,4096]{2,1,0:T(8,128)} %get-tuple-element.9) | copy-start | bytes 6291460

commit v3 on v2

--- a/solution.py
+++ b/solution.py
@@ -1,4 +1,3 @@
-import functools
 import math
 
 import jax
@@ -124,6 +123,7 @@
 F32 = jnp.float32
 BF16 = jnp.bfloat16
 STEP = 512
+LAST_STEPS = 4
 HALF_LOG2_E = 0.5 / math.log(2.0)
 
 
@@ -151,7 +151,7 @@
 def fused_kernel(
     x_hbm, ct_hbm, w_hbm, w_in, b_in, w_out_t, b_out,
     kz, kz_t, ky, ky_t, kx, kx_t, spread, spread_t,
-    gx_hbm, gw_hbm,
+    part_hbm, kept_hbm, gw_hbm,
     x_v, ct_v, w_v, gw_v, slope_v, part_v, gp_v, along_z, rows_v,
     send_s, recv_s, send_g, recv_g, wide_v, first_v, w_out, bias_v,
     send_sem, recv_sem, load_sem, store_sem,
@@ -272,15 +272,20 @@
             part_v[u] = dot(w_out_t[...], act * phi) + jnp.concatenate([bias_v[...]] * 4, axis=1)
             return carry
 
-        lax.fori_loop(first, last, unit, 0, unroll=2)
+        lax.fori_loop(first, last, unit, 0, unroll=4)
 
     def backward_units(first, last):
         def unit(u, carry):
             grad = dot(w_out[...], gp_v[u]).astype(BF16) * slope_v[u]
-            part_v[u] = dot(w_in[...], grad)
+            gp_v[u] = dot(w_in[...], grad).astype(BF16)
             return carry
 
-        lax.fori_loop(first, last, unit, 0, unroll=4)
+        lax.fori_loop(first, last, unit, 0, unroll=8)
+
+        span = pl.ds(first, last - first)
+        store = pltpu.make_async_copy(gp_v.at[span], part_hbm.at[span], store_sem.at[first // 16])
+        store.start()
+        return store
 
     loads[0].wait()
 
@@ -321,7 +326,7 @@
                 return total + sum(term[:, q * 128 : (q + 1) * 128] for q in range(STEP // 128))
 
             total = lax.fori_loop(
-                0, C * C // STEP, mix, jnp.zeros((GROUPS * GM, 2 * C), F32), unroll=4
+                0, C * C // STEP, mix, jnp.zeros((GROUPS * GM, 2 * C), F32), unroll=8
             )
             mixed.append(total[:, :C] + total[:, C:])
         send_g[1, :, :, 2 * p * C : 2 * (p + 1) * C] = (
@@ -352,10 +357,10 @@
 
     lax.fori_loop(0, XL, middle_plane, 0)
     flight = send_along_y(4)
-    backward_units(0, 16)
+    stores = [backward_units(0, 16)]
     finish(flight)
     flight = send_modes(5)
-    backward_units(16, 32)
+    stores.append(backward_units(16, 32))
     finish(flight)
 
     for p in range(JL // 2):
@@ -374,7 +379,7 @@
 
             mixed.append(
                 lax.fori_loop(
-                    0, C * C // STEP, mix_back, jnp.zeros((GROUPS * GM, C), F32), unroll=4
+                    0, C * C // STEP, mix_back, jnp.zeros((GROUPS * GM, C), F32), unroll=8
                 )
             )
         send_g[3, :, :, 2 * p * C : 2 * (p + 1) * C] = (
@@ -395,45 +400,48 @@
                 gw_v[jl, :, span] = jnp.sum(left * wide, axis=0)
                 return carry
 
-            lax.fori_loop(0, C * C // 128, outer, 0, unroll=4)
-    store_gw = pltpu.make_async_copy(gw_v, gw_hbm, store_sem.at[0])
-    store_gw.start()
+            lax.fori_loop(0, C * C // 128, outer, 0, unroll=8)
+    stores.append(pltpu.make_async_copy(gw_v, gw_hbm, store_sem.at[3]))
+    stores[-1].start()
     finish(flight)
     flight = send_planes(7)
-    backward_units(32, UNITS)
+    stores.append(backward_units(32, UNITS))
     finish(flight)
     back_along_y(7)
 
-    def last_plane(xl, carry):
+    stores.append(pltpu.make_async_copy(along_z, kept_hbm, store_sem.at[4]))
+    stores[-1].start()
+    for store in stores:
+        store.wait()
+
+
+def last_kernel(part, kept, weight_grad, kz, field_out, weight_out):
+    weight_out[...] = weight_grad[...]
+    for xl in range(XL // LAST_STEPS):
         for t in range(NY // 8):
-            kept = along_z[plane_rows(xl), t * 128 : (t + 1) * 128]
+            rows = kept[xl * C : (xl + 1) * C, t * 128 : (t + 1) * 128]
             u = xl * (NY // 4) + 2 * t
-            total = jnp.concatenate([part_v[u], part_v[u + 1]], axis=1)
-            total = (total + dot(kept, kz[...]) * FACTOR).astype(BF16)
+            total = jnp.concatenate([part[u], part[u + 1]], axis=1).astype(F32)
+            total = (total + dot(rows, kz[...]) * FACTOR).astype(BF16)
             for q in range(8):
-                ct_v[xl * NY + t * 8 + q] = total[:, q * NZ : (q + 1) * NZ]
-        return carry
-
-    lax.fori_loop(0, XL, last_plane, 0)
-    store_gx = pltpu.make_async_copy(ct_v, gx_hbm, store_sem.at[1])
-    store_gx.start()
-    store_gw.wait()
-    store_gx.wait()
+                field_out[xl * NY + t * 8 + q] = total[:, q * NZ : (q + 1) * NZ]
 
 
 def fused_device(inputs, cotangent, spectral_weight, w_in, b_in, w_out, b_out):
     field = inputs.shape
     flat = (XL * NY, C, NZ)
+    tables = host_tables()
     any_spec = pl.BlockSpec(memory_space=pl.ANY)
     vmem_spec = pl.BlockSpec(memory_space=pltpu.VMEM)
-    out = pl.pallas_call(
+    part, kept, weight_grad = pl.pallas_call(
         fused_kernel,
         out_shape=(
-            jax.ShapeDtypeStruct(flat, BF16),
+            jax.ShapeDtypeStruct((UNITS, C, 4 * NZ), BF16),
+            jax.ShapeDtypeStruct((XL * C, NY * MZ), BF16),
             jax.ShapeDtypeStruct((JL, GM, C * C), F32),
         ),
         in_specs=[any_spec] * 3 + [vmem_spec] * 12,
-        out_specs=(any_spec, any_spec),
+        out_specs=(any_spec,) * 3,
         scratch_shapes=[
             pltpu.VMEM(flat, BF16),
             pltpu.VMEM(flat, BF16),
@@ -455,16 +463,35 @@
             pltpu.SemaphoreType.DMA((8, GROUPS - 1)),
             pltpu.SemaphoreType.DMA((8, GROUPS - 1)),
             pltpu.SemaphoreType.DMA((3,)),
-            pltpu.SemaphoreType.DMA((2,)),
+            pltpu.SemaphoreType.DMA((5,)),
         ],
         compiler_params=pltpu.CompilerParams(
             collective_id=0, has_side_effects=True, vmem_limit_bytes=60 * 1024 * 1024
         ),
     )(
         inputs.reshape(flat), cotangent.reshape(flat), spectral_weight,
-        w_in, b_in[None], w_out.T, b_out[None], *host_tables(),
-    )
-    return out[0].reshape(field), out[1]
+        w_in, b_in[None], w_out.T, b_out[None], *tables,
+    )
+    blocks = (
+        pl.BlockSpec((UNITS // LAST_STEPS, C, 4 * NZ), lambda n: (n, 0, 0)),
+        pl.BlockSpec((XL * C // LAST_STEPS, NY * MZ), lambda n: (n, 0)),
+        pl.BlockSpec((JL // LAST_STEPS, GM, C * C), lambda n: (n, 0, 0)),
+        pl.BlockSpec((8 * MZ, 8 * NZ), lambda n: (0, 0)),
+        pl.BlockSpec((XL * NY // LAST_STEPS, C, NZ), lambda n: (n, 0, 0)),
+        pl.BlockSpec((JL // LAST_STEPS, GM, C * C), lambda n: (n, 0, 0)),
+    )
+    grad_field, weight_grad = pl.pallas_call(
+        last_kernel,
+        grid=(LAST_STEPS,),
+        out_shape=(
+            jax.ShapeDtypeStruct(flat, BF16),
+            jax.ShapeDtypeStruct((JL, GM, C * C), F32),
+        ),
+        in_specs=list(blocks[:4]),
+        out_specs=blocks[4:],
+        compiler_params=pltpu.CompilerParams(vmem_limit_bytes=60 * 1024 * 1024),
+    )(part, kept, weight_grad, tables[0])
+    return grad_field.reshape(field), weight_grad
 
 
 def solution(mesh):

time: 75.4 us -> 69.7 us (0.924)
  local copies, waits for them, and re-layouts: 5.92 us -> 0 us
    unnamed x4 -> x0, local copies, waits for them, and re-layouts: 5.92 us -> none
    pallas_call x1 -> x2, Pallas kernels: 68.7 us -> 68.8 us  [the longest x1 62.8 us: fused_device(): pl.pallas_call(fused_kernel, out_shape=(jax.ShapeDtypeStruct((UNITS, C, 4...]
where the time goes in v3:
time: 69.7 us; the launch traced here: 69.4 us
  Pallas kernels  68.8 us (99%)
    pallas_call x1, Pallas kernels, fused_device(): pl.pallas_call(fused_kernel, out_shape=(jax.ShapeDtypeStruct((UNITS, C, 4...  62.8 us
    pallas_call x1, Pallas kernels, fused_device(): pl.pallas_call(last_kernel, grid=(LAST_STEPS,), out_shape=(jax.ShapeDtype...  5.95 us

profile of v3, /device:TPU:0, one launch (start us, length us, event | category | flops | bytes accessed | tf_op | source)
XLA Modules:
  0.0 69.4 jit_solution(8725461753685471973)
XLA Ops:
  0.6 62.8 %shard_map.158 = (bf16[48,64,512]{2,1,0:T(8,128)(2,1)}, bf16[512,384]{1,0:T(8,128)(2,1)}, f32[4,32,4096]{2,1,0:T(8,128)}) custom-call(bf16[192,64,128]{2,1,0:T(8,128)(2,1)} %bitcast.6, bf16[192,64,128]{2,1,0:T(8,128)(2,1)} %bitcast.7, bf16[4,32,4096]{2,1,0:T(8,128)(2,1)} %w_hbm.1, bf16[64,256]{1,0:T(8,128)(2,1)} %w_in.1, f32[1,256]{1,0:T(1,128)} %bitcast.9, ...), custom_call_target="tpu_custom_call" | custom-call | tf_op jit(solution)/shard_map/pallas_call | solution.py:436
  63.5 5.9 %shard_map.159 = (bf16[192,64,128]{2,1,0:T(8,128)(2,1)}, f32[4,32,4096]{2,1,0:T(8,128)}) custom-call(bf16[48,64,512]{2,1,0:T(8,128)(2,1)} %get-tuple-element.7.part, bf16[512,384]{1,0:T(8,128)(2,1)} %get-tuple-element.8.kept, f32[4,32,4096]{2,1,0:T(8,128)} %get-tuple-element.9.weight_grad, bf16[128,1024]{1,0:T(8,128)(2,1)} %constant.16.clone.kz), custom_call_target="tpu_custom_call" | custom-call | tf_op jit(solution)/shard_map/pallas_call | solution.py:483

commit v4 on v3

--- a/solution.py
+++ b/solution.py
@@ -347,9 +347,10 @@
             kept = along_z[plane_rows(xl), t * 128 : (t + 1) * 128]
             u = xl * (NY // 4) + 2 * t
             pre = jnp.concatenate([part_v[u], part_v[u + 1]], axis=1) + dot(kept, kz[...]) * FACTOR
+            pre = pre.astype(BF16)
             phi = 0.5 + 0.5 * lax.erf(pre * root_half)
-            slope = phi + pre * jnp.exp(pre * pre * -0.5) * inv_root_two_pi
-            grad = (lanes_of(ct_v, xl, t * 8, 8).astype(F32) * slope).astype(BF16)
+            slope = phi + pre * (jnp.exp2(pre * pre * -HALF_LOG2_E) * inv_root_two_pi)
+            grad = lanes_of(ct_v, xl, t * 8, 8) * slope
             gp_v[u] = grad[:, :512]
             gp_v[u + 1] = grad[:, 512:]
             along_z[plane_rows(xl), t * 128 : (t + 1) * 128] = dot(grad, kz_t[...]).astype(BF16)

time: 69.7 us -> 68.3 us (0.980)
  Pallas kernels: 68.8 us -> 67.4 us
    pallas_call x1, Pallas kernels: 62.8 us -> 61.4 us  [fused_device(): pl.pallas_call(fused_kernel, out_shape=(jax.ShapeDtypeStruct((UNITS, C, 4...]
where the time goes in v4:
time: 68.3 us; the launch traced here: 68 us
  Pallas kernels  67.4 us (99%)
    pallas_call x1, Pallas kernels, fused_device(): pl.pallas_call(fused_kernel, out_shape=(jax.ShapeDtypeStruct((UNITS, C, 4...  61.4 us
    pallas_call x1, Pallas kernels, fused_device(): pl.pallas_call(last_kernel, grid=(LAST_STEPS,), out_shape=(jax.ShapeDtype...  5.95 us

profile of v4, /device:TPU:0, one launch (start us, length us, event | category | flops | bytes accessed | tf_op | source)
XLA Modules:
  0.0 68.0 jit_solution(8179297305219908497)
XLA Ops:
  0.6 61.4 %shard_map.158 = (bf16[48,64,512]{2,1,0:T(8,128)(2,1)}, bf16[512,384]{1,0:T(8,128)(2,1)}, f32[4,32,4096]{2,1,0:T(8,128)}) custom-call(bf16[192,64,128]{2,1,0:T(8,128)(2,1)} %bitcast.6, bf16[192,64,128]{2,1,0:T(8,128)(2,1)} %bitcast.7, bf16[4,32,4096]{2,1,0:T(8,128)(2,1)} %w_hbm.1, bf16[64,256]{1,0:T(8,128)(2,1)} %w_in.1, f32[1,256]{1,0:T(1,128)} %bitcast.9, ...), custom_call_target="tpu_custom_call" | custom-call | tf_op jit(solution)/shard_map/pallas_call | solution.py:437
  62.0 5.9 %shard_map.159 = (bf16[192,64,128]{2,1,0:T(8,128)(2,1)}, f32[4,32,4096]{2,1,0:T(8,128)}) custom-call(bf16[48,64,512]{2,1,0:T(8,128)(2,1)} %get-tuple-element.7.part, bf16[512,384]{1,0:T(8,128)(2,1)} %get-tuple-element.8.kept, f32[4,32,4096]{2,1,0:T(8,128)} %get-tuple-element.9.weight_grad, bf16[128,1024]{1,0:T(8,128)(2,1)} %constant.16.clone.kz), custom_call_target="tpu_custom_call" | custom-call | tf_op jit(solution)/shard_map/pallas_call | solution.py:484
